TPU v7x, 512 devices: a whole 4x8x8 slice. The times are simulated.
512 devices in a mesh: seq: 32 (over z_hi, y, core), tensor: 16 (over x, z_lo).
Axes of the slice: x: 4, y: 8, z: 8 (z_hi: 2, z_lo: 4; z = z_hi * 4 + z_lo), core: 2. Of those that a mesh axis runs over, the one named last changes fastest.
Arguments:
- hidden_in: bfloat16 [8192, 5376], P('seq', 'tensor'), may hold values from -128 to 128
- positions: int32 [8192], P('seq'), may hold values from 0 to 16382, as said below
- pre_gain: float32 [5376], replicated, may hold values from -0.5 to 1.5
- query_weight: bfloat16 [5376, 4096], P('seq', 'tensor')
- key_weight: bfloat16 [5376, 2048], P('seq', 'tensor')
- value_weight: bfloat16 [5376, 2048], P('seq', 'tensor'), may hold values from -0.078125 to 0.078125
- query_gain: float32 [128], replicated, may hold values from -0.3 to 4.5
- key_gain: float32 [128], replicated, may hold values from -0.3 to 4.5
- output_weight: bfloat16 [4096, 5376], P('tensor', 'seq')
- post_gain: float32 [5376], P('tensor'), may hold values from -0.5 to 1.5
Outputs:
- hidden_out: bfloat16 [8192, 5376], P('seq', 'tensor')
Inputs may be any that keep to these rules, and one draw needn't show every extreme that they name: `positions`: 0 at a prompt's first token, else one more than the position of the token before; the window's first token continues a prompt begun before the window, and some later token starts a new prompt.
All inputs are finite; a program needn't handle non-finite values.
Results may differ from a plain program's by a relative error of at most 0.013.
Values may be sent and summed in bfloat16 or wider, within the bound.
A program may use at most 64 MiB of HBM per device.

v0:
```python
import jax
import jax.numpy as jnp
from jax import lax
from jax.sharding import PartitionSpec as P

WINDOW = 1024
epsilon = 1e-06
query_scalar = 168.0
rope_base = 10000.0
masked_score = -1e30


def passed_along(value, axis, steps):
    count = lax.axis_size(axis)
    initial, last = (max(0, -steps), min(count, count - steps))
    return lax.ppermute(value, axis, [(source, source + steps) for source in range(initial, last)])


def rms_scale(values):
    return values * lax.rsqrt(jnp.mean(values * values, axis=-1, keepdims=True) + epsilon)


def rotary(values, token_positions):
    half_dim = values.shape[-1] // 2
    exponent = jnp.arange(half_dim, dtype=jnp.float32) * 2.0 / values.shape[-1]
    inverse = 1.0 / rope_base**exponent
    angles = token_positions.astype(jnp.float32)[:, None] * inverse[None, :]
    cosine = jnp.cos(angles)[:, None, :]
    sine = jnp.sin(angles)[:, None, :]
    first_half = values[..., :half_dim]
    second_half = values[..., half_dim:]
    return jnp.concatenate(
        [first_half * cosine - second_half * sine, second_half * cosine + first_half * sine],
        axis=-1,
    )


def body(
    hidden_in,
    positions,
    pre_gain,
    query_weight,
    key_weight,
    value_weight,
    query_gain,
    key_gain,
    output_weight,
    post_gain,
):
    tokens_dev = hidden_in.shape[0]
    width_dev = hidden_in.shape[1]
    head_dim = query_gain.shape[0]
    kv_local = key_weight.shape[1] // head_dim
    whole = lax.all_gather(hidden_in, "tensor", axis=1, tiled=True)
    normed = (rms_scale(whole.astype(jnp.float32)) * (1.0 + pre_gain)).astype(jnp.bfloat16)

    def accumulate(piece):
        return jnp.dot(normed, piece, preferred_element_type=jnp.float32)

    query_sum = accumulate(lax.all_gather(query_weight, "seq", axis=0, tiled=True))
    key_sum = accumulate(lax.all_gather(key_weight, "seq", axis=0, tiled=True))
    value_sum = accumulate(lax.all_gather(value_weight, "seq", axis=0, tiled=True))
    queries = rotary(
        rms_scale(query_sum.reshape(tokens_dev, -1, head_dim)) * (1.0 + query_gain), positions
    )
    queries = queries.astype(jnp.bfloat16).reshape(tokens_dev, kv_local, 2, head_dim)
    key_own = rotary(
        rms_scale(key_sum.reshape(tokens_dev, kv_local, head_dim)) * (1.0 + key_gain), positions
    ).astype(jnp.bfloat16)
    value_own = value_sum.reshape(tokens_dev, kv_local, head_dim).astype(jnp.bfloat16)
    reach = (WINDOW + tokens_dev - 2) // tokens_dev
    earlier = []
    for distance in range(reach, 0, -1):
        earlier.append(passed_along((key_own, value_own), "seq", distance))
    key_rows = jnp.concatenate([pair[0] for pair in earlier] + [key_own], axis=0)
    value_rows = jnp.concatenate([pair[1] for pair in earlier] + [value_own], axis=0)
    seq_index = lax.axis_index("seq")
    query_index = seq_index * tokens_dev + jnp.arange(tokens_dev, dtype=jnp.int32)
    key_index = (seq_index - reach) * tokens_dev + jnp.arange(key_rows.shape[0], dtype=jnp.int32)
    gap = query_index[:, None] - key_index[None, :]
    allowed = (gap >= 0) & (gap < WINDOW) & (gap <= positions[:, None]) & (key_index >= 0)[None, :]
    scores = jnp.einsum(
        "qgrd,kgd->grqk", queries, key_rows, preferred_element_type=jnp.float32
    ) * query_scalar ** (-0.5)
    scores = jnp.where(allowed[None, None], scores, masked_score)
    peak = jnp.max(scores, axis=-1, keepdims=True)
    expo = jnp.exp(scores - peak)
    weights = (expo / jnp.sum(expo, axis=-1, keepdims=True)).astype(jnp.bfloat16)
    context = jnp.einsum("grqk,kgd->qgrd", weights, value_rows, preferred_element_type=jnp.float32)
    context = context.astype(jnp.bfloat16).reshape(tokens_dev, -1)
    term = jnp.dot(
        context,
        lax.all_gather(output_weight, "seq", axis=1, tiled=True),
        preferred_element_type=jnp.float32,
    )
    share = lax.psum_scatter(
        term.astype(jnp.bfloat16), "tensor", scatter_dimension=1, tiled=True
    ).astype(jnp.float32)
    squares = lax.psum(jnp.sum(share * share, axis=-1), "tensor")
    mean_square = squares / (width_dev * lax.axis_size("tensor"))
    post = share * lax.rsqrt(mean_square[:, None] + epsilon) * (1.0 + post_gain)
    return (hidden_in.astype(jnp.float32) + post).astype(jnp.bfloat16)


def solution(mesh):
    placed = (
        P("seq", "tensor"),
        P("seq"),
        P(),
        P("seq", "tensor"),
        P("seq", "tensor"),
        P("seq", "tensor"),
        P(),
        P(),
        P("tensor", "seq"),
        P("tensor"),
    )
    return jax.shard_map(
        body, mesh=mesh, in_specs=placed, out_specs=P("seq", "tensor"), check_vma=False
    )
```

profile of v0, /device:TPU:16, one launch (start us, length us, event | category | flops | bytes accessed | tf_op | source)
XLA Modules:
  0.0 622.8 jit_solution(4040736795534656457)
XLA Ops:
  13.3 1.6 fusion.10
  14.9 93.1 %all-gather.6.cloned.1.call-done = bf16[256,5376]{0,1:T(8,128)(2,1)} async-done(((bf16[256,336]{0,1:T(8,128)(2,1)}), bf16[256,5376]{0,1:T(8,128)(2,1)}) %all-gather.6.cloned.1.call-update) | async-done | bytes 2752528 | tf_op jit(solution)/shard_map/all_gather | solution.py:54
  108.0 2.7 fusion
  110.7 87.3 %all-gather.10.cloned.1.call-done = bf16[5376,128]{1,0:T(8,128)(2,1)} async-done(((bf16[168,128]{1,0:T(8,128)(2,1)}), bf16[5376,128]{1,0:T(8,128)(2,1)}) %all-gather.10.cloned.1.call-update) | async-done | bytes 1376272 | tf_op jit(solution)/shard_map/all_gather | solution.py:61
  197.9 2.7 multiply_reduce_fusion.1
  201.1 3.8 collective-permute-start.4
  204.9 2.8 collective-permute-start.5
  207.7 3.4 collective-permute-start.6
  211.1 2.3 collective-permute-start.7
  213.4 73.1 %all-gather.8.cloned.1.call-done = bf16[5376,128]{1,0:T(8,128)(2,1)} async-done(((bf16[168,128]{1,0:T(8,128)(2,1)}), bf16[5376,128]{1,0:T(8,128)(2,1)}) %all-gather.8.cloned.1.call-update) | async-done | bytes 1376272 | tf_op jit(solution)/shard_map/all_gather | solution.py:62
  286.6 3.1 fusion.14
  289.6 3.8 collective-permute-start
  293.4 2.8 collective-permute-start.1
  297.7 3.4 collective-permute-start.2
  302.6 2.3 collective-permute-start.3
  310.8 71.3 %all-gather.12.cloned.1.call-done = bf16[5376,256]{1,0:T(8,128)(2,1)} async-done(((bf16[168,256]{1,0:T(8,128)(2,1)}), bf16[5376,256]{1,0:T(8,128)(2,1)}) %all-gather.12.cloned.1.call-update) | async-done | bytes 2752528 | tf_op jit(solution)/shard_map/all_gather | solution.py:60
  382.1 4.2 multiply_reduce_fusion
  387.7 1.6 fusion.38
  389.7 1.6 fusion.11
  391.3 85.6 %all-gather.14.cloned.1.call-done = bf16[256,5376]{0,1:T(8,128)(2,1)} async-done(((bf16[256,168]{0,1:T(8,128)(2,1)}), bf16[256,5376]{0,1:T(8,128)(2,1)}) %all-gather.14.cloned.1.call-update) | async-done | bytes 2752528 | tf_op jit(solution)/shard_map/all_gather | solution.py:93
  476.9 4.2 convolution_convert_fusion
  481.8 91.6 %reduce-scatter.2.cloned.1.call-done = bf16[256,336]{0,1:T(8,128)(2,1)} async-done(((bf16[256,5376]{0,1:T(8,128)(2,1)}), bf16[256,336]{0,1:T(8,128)(2,1)}) %reduce-scatter.2.cloned.1.call-update) | async-done | bytes 172048 | tf_op jit(solution)/shard_map/reduce_scatter | solution.py:96
  574.4 39.8 %psum.7 = f32[256]{0:T(256)S(1)} all-reduce(f32[256]{0:T(256)S(1)} %fusion.15), channel_id=1, replica_groups=mesh['seq'=32,'tensor'=16] {'tensor'}, use_global_device_ids=true, to_apply=%region_7.8 | all-reduce | flops 256 | bytes 2048 | tf_op jit(solution)/shard_map/psum | solution.py:99
  614.2 1.7 fusion.18
  (60 shorter events, 19.4 us)
Async XLA Ops:
  6.5 101.5 %all-gather.6.cloned.1.call-start = ((), (), s32[]{:S(2)}) async-start(), calls=%async_computation.1 | async-start | bytes 2924544 | tf_op jit(solution)/shard_map/all_gather | solution.py:54
  7.3 190.7 %all-gather.10.cloned.1.call-start = ((), (), s32[]{:S(2)}) async-start(), calls=%async_computation.3 | async-start | bytes 1419264 | tf_op jit(solution)/shard_map/all_gather | solution.py:61
  8.0 278.6 %all-gather.8.cloned.1.call-start = ((), (), s32[]{:S(2)}) async-start(), calls=%async_computation.2 | async-start | bytes 1419264 | tf_op jit(solution)/shard_map/all_gather | solution.py:62
  8.7 373.4 %all-gather.12.cloned.1.call-start = ((), (), s32[]{:S(2)}) async-start(), calls=%async_computation.4 | async-start | bytes 2838528 | tf_op jit(solution)/shard_map/all_gather | solution.py:60
  9.3 467.6 %all-gather.14.cloned.1.call-start = ((), (), s32[]{:S(2)}) async-start(), calls=%async_computation.5 | async-start | bytes 2838528 | tf_op jit(solution)/shard_map/all_gather | solution.py:93
  9.9 563.5 %reduce-scatter.2.cloned.1.call-start = ((), (), s32[]{:S(2)}) async-start(), calls=%async_computation.6 | async-start | bytes 2924544 | tf_op jit(solution)/shard_map/reduce_scatter | solution.py:96
  10.7 189.9 %copy-start.2 = (f32[5376]{0:T(1024)}, f32[5376]{0:T(1024)S(1)}, u32[]{:S(2)}) copy-start(f32[5376]{0:T(1024)S(1)} %broadcast_add_fusion) | copy-start | bytes 64516
  108.0 89.9 %copy-start = (bf16[256,5376]{0,1:T(8,128)(2,1)S(1)}, bf16[256,5376]{0,1:T(8,128)(2,1)}, u32[]{:S(2)}) copy-start(bf16[256,5376]{0,1:T(8,128)(2,1)} %all-gather.6.cloned.1.call-done) | copy-start | bytes 8257540
  201.1 92.3 %collective-permute-start.4 = (bf16[256,1,128]{0,2,1:T(8,128)(2,1)S(1)}, bf16[256,1,128]{0,2,1:T(8,128)(2,1)}, u32[]{:S(2)}, u32[]{:S(2)}) collective-permute-start(bf16[256,1,128]{0,2,1:T(8,128)(2,1)S(1)} %pad_maximum_fusion), channel_id=1, source_target_pairs={{0,64},{16,80},{32,96},{48,112},{64,128},{80,144},{96,160},{112,17... | collective-permute-start | bytes 196616 | tf_op jit(solution)/shard_map/ppermute | solution.py:16
  204.9 92.8 %collective-permute-start.5 = (bf16[256,1,128]{0,2,1:T(8,128)(2,1)S(1)}, bf16[256,1,128]{0,2,1:T(8,128)(2,1)}, u32[]{:S(2)}, u32[]{:S(2)}) collective-permute-start(bf16[256,1,128]{0,2,1:T(8,128)(2,1)S(1)} %pad_maximum_fusion), channel_id=1, source_target_pairs={{0,48},{16,64},{32,80},{48,96},{64,112},{80,128},{96,144},{112,160... | collective-permute-start | bytes 196616 | tf_op jit(solution)/shard_map/ppermute | solution.py:16
  207.7 94.9 %collective-permute-start.6 = (bf16[256,1,128]{0,2,1:T(8,128)(2,1)S(1)}, bf16[256,1,128]{0,2,1:T(8,128)(2,1)}, u32[]{:S(2)}, u32[]{:S(2)}) collective-permute-start(bf16[256,1,128]{0,2,1:T(8,128)(2,1)S(1)} %pad_maximum_fusion), channel_id=1, source_target_pairs={{0,32},{16,48},{32,64},{48,80},{64,96},{80,112},{96,128},{112,144}... | collective-permute-start | bytes 196616 | tf_op jit(solution)/shard_map/ppermute | solution.py:16
  211.1 95.2 %collective-permute-start.7 = (bf16[256,1,128]{0,2,1:T(8,128)(2,1)S(1)}, bf16[256,1,128]{0,2,1:T(8,128)(2,1)S(1)}, u32[]{:S(2)}, u32[]{:S(2)}) collective-permute-start(bf16[256,1,128]{0,2,1:T(8,128)(2,1)S(1)} %pad_maximum_fusion), channel_id=1, source_target_pairs={{0,16},{16,32},{32,48},{48,64},{64,80},{80,96},{96,112},{112,128},... | collective-permute-start | bytes 196616 | tf_op jit(solution)/shard_map/ppermute | solution.py:16
  289.6 18.0 %collective-permute-start = (bf16[256,1,128]{2,0,1:T(8,128)(2,1)S(1)}, bf16[256,1,128]{2,0,1:T(8,128)(2,1)S(1)}, u32[]{:S(2)}, u32[]{:S(2)}) collective-permute-start(bf16[256,1,128]{2,0,1:T(8,128)(2,1)S(1)} %fusion.14), channel_id=1, source_target_pairs={{0,64},{16,80},{32,96},{48,112},{64,128},{80,144},{96,160},{112,17... | collective-permute-start | bytes 196616 | tf_op jit(solution)/shard_map/ppermute | solution.py:16
  293.4 14.9 %collective-permute-start.1 = (bf16[256,1,128]{2,0,1:T(8,128)(2,1)S(1)}, bf16[256,1,128]{2,0,1:T(8,128)(2,1)S(1)}, u32[]{:S(2)}, u32[]{:S(2)}) collective-permute-start(bf16[256,1,128]{2,0,1:T(8,128)(2,1)S(1)} %fusion.14), channel_id=1, source_target_pairs={{0,48},{16,64},{32,80},{48,96},{64,112},{80,128},{96,144},{112,160... | collective-permute-start | bytes 196616 | tf_op jit(solution)/shard_map/ppermute | solution.py:16
  297.7 11.2 %collective-permute-start.2 = (bf16[256,1,128]{2,0,1:T(8,128)(2,1)S(1)}, bf16[256,1,128]{2,0,1:T(8,128)(2,1)S(1)}, u32[]{:S(2)}, u32[]{:S(2)}) collective-permute-start(bf16[256,1,128]{2,0,1:T(8,128)(2,1)S(1)} %fusion.14), channel_id=1, source_target_pairs={{0,32},{16,48},{32,64},{48,80},{64,96},{80,112},{96,128},{112,144}... | collective-permute-start | bytes 196616 | tf_op jit(solution)/shard_map/ppermute | solution.py:16
  302.6 6.9 %collective-permute-start.3 = (bf16[256,1,128]{2,0,1:T(8,128)(2,1)S(1)}, bf16[256,1,128]{2,0,1:T(8,128)(2,1)S(1)}, u32[]{:S(2)}, u32[]{:S(2)}) collective-permute-start(bf16[256,1,128]{2,0,1:T(8,128)(2,1)S(1)} %fusion.14), channel_id=1, source_target_pairs={{0,16},{16,32},{32,48},{48,64},{64,80},{80,96},{96,112},{112,128},... | collective-permute-start | bytes 196616 | tf_op jit(solution)/shard_map/ppermute | solution.py:16
  481.2 0.7 copy-start.3
  481.2 133.1 %copy-start.1 = (bf16[256,336]{0,1:T(8,128)(2,1)S(1)}, bf16[256,336]{0,1:T(8,128)(2,1)}, u32[]{:S(2)}) copy-start(bf16[256,336]{0,1:T(8,128)(2,1)} %param.10) | copy-start | bytes 516100
Sparse Core Ops, SparseCore 0:
  9.4 98.5 all-gather.5
  111.2 86.6 all-gather.9
  201.2 85.3 all-gather.7
  289.6 92.4 all-gather.11
  385.2 91.6 all-gather.13
  481.3 92.0 reduce-scatter.1
where the time goes:
time: 624 us; the launch traced here: 623 us
  waiting for transfers between devices  505 us (81%)
  blocking collectives  39.8 us (6%)
  starting transfers between devices  24.7 us (4%)
  matrix products  17.4 us (3%)
  between operations  13.7 us (2%)
  other arithmetic  12 us (2%)
  local copies, waits for them, and re-layouts  10 us (2%)
    all_gather x1, waiting for transfers between devices, body(): whole = lax.all_gather(hidden_in, 'tensor', axis=1, tiled=True)  93.1 us
    reduce_scatter x1, waiting for transfers between devices, body(): lax.psum_scatter(term.astype(jnp.bfloat16), 'tensor', scatter_dimension=1...  91.6 us
    all_gather x1, waiting for transfers between devices, body(): key_sum = accumulate(lax.all_gather(key_weight, 'seq', axis=0, tiled=True))  87.3 us
    all_gather x1, waiting for transfers between devices, body(): lax.all_gather(output_weight, 'seq', axis=1, tiled=True)  85.6 us
    all_gather x1, waiting for transfers between devices, body(): lax.all_gather(value_weight, 'seq', axis=0, tiled=True)  73.1 us
    all_gather x1, waiting for transfers between devices, body(): lax.all_gather(query_weight, 'seq', axis=0, tiled=True)  71.3 us
    psum x1, blocking collectives, body(): squares = lax.psum(jnp.sum(share * share, axis=-1), 'tensor')  39.8 us
    ppermute x8, starting transfers between devices, passed_along(): lax.ppermute(value, axis, [(source, source + steps) for source in range(i...  24.5 us
  transfers between devices with their start and end apart: 14, of which 6 were waited for; matrix products, arithmetic and copies ran while one was open for 5% of the time, Pallas kernels for 0%

commit v1 on v0

--- a/solution.py
+++ b/solution.py
@@ -57,7 +57,11 @@
     def accumulate(piece):
         return jnp.dot(normed, piece, preferred_element_type=jnp.float32)
 
-    query_sum = accumulate(lax.all_gather(query_weight, "seq", axis=0, tiled=True))
+    query_sum = accumulate(
+        jnp.concatenate(
+            lax.all_to_all(jnp.stack([query_weight] * lax.axis_size("seq")), "seq", 0, 0), axis=0
+        )
+    )
     key_sum = accumulate(lax.all_gather(key_weight, "seq", axis=0, tiled=True))
     value_sum = accumulate(lax.all_gather(value_weight, "seq", axis=0, tiled=True))
     queries = rotary(

time: 624 us -> 591 us (0.947)
  the two profiles are of different devices: /device:TPU:16 before, /device:TPU:32 now
where the time goes in v1:
time: 591 us
  waiting for transfers between devices  464 us (79%)
  blocking collectives  40.5 us (7%)
  starting transfers between devices  37.3 us (6%)
  matrix products  17.5 us (3%)
  between operations  13.5 us (2%)
  local copies, waits for them, and re-layouts  10.4 us (2%)
  other arithmetic  7.47 us (1%)
    all_gather x1, waiting for transfers between devices, body(): whole = lax.all_gather(hidden_in, 'tensor', axis=1, tiled=True)  138 us
    reduce_scatter x1, waiting for transfers between devices, body(): lax.psum_scatter(term.astype(jnp.bfloat16), 'tensor', scatter_dimension=1...  92.8 us
    all_gather x1, waiting for transfers between devices, body(): key_sum = accumulate(lax.all_gather(key_weight, 'seq', axis=0, tiled=True))  85.9 us
    all_gather x1, waiting for transfers between devices, body(): lax.all_gather(value_weight, 'seq', axis=0, tiled=True)  74.8 us
    all_gather x1, waiting for transfers between devices, body(): lax.all_gather(output_weight, 'seq', axis=1, tiled=True)  67.2 us
    psum x1, blocking collectives, body(): squares = lax.psum(jnp.sum(share * share, axis=-1), 'tensor')  40.5 us
    ppermute x8, starting transfers between devices, passed_along(): lax.ppermute(value, axis, [(source, source + steps) for source in range(i...  21.2 us
    all_to_all x1, starting transfers between devices, body(): lax.all_to_all(jnp.stack([query_weight] * lax.axis_size('seq')), 'seq', 0...  16 us
  transfers between devices with their start and end apart: 14, of which 8 were waited for; matrix products, arithmetic and copies ran while one was open for 5% of the time, Pallas kernels for 0%

profile of v1, /device:TPU:32, one launch (start us, length us, event | category | flops | bytes accessed | tf_op | source)
XLA Modules:
  0.0 590.8 jit_solution(18371298373084979569)
XLA Ops:
  8.7 2.6 stack.2
  11.4 16.0 %all-to-all-start = ((bf16[32,168,256]{2,1,0:T(8,128)(2,1)}), bf16[32,168,256]{2,1,0:T(8,128)(2,1)S(1)}, u32[]{:S(2)}, u32[]{:S(2)}) async-start(bf16[32,168,256]{2,1,0:T(8,128)(2,1)} %stack.2), calls=%async_computation | async-start | bytes 5505024 | tf_op jit(solution)/shard_map/all_to_all | solution.py:62
  29.4 137.9 %all-gather.5.cloned.1.call-done = bf16[256,5376]{0,1:T(8,128)(2,1)} async-done(((bf16[256,336]{0,1:T(8,128)(2,1)}), bf16[256,5376]{0,1:T(8,128)(2,1)}) %all-gather.5.cloned.1.call-update) | async-done | bytes 2752528 | tf_op jit(solution)/shard_map/all_gather | solution.py:54
  167.3 2.5 fusion
  169.8 85.9 %all-gather.9.cloned.1.call-done = bf16[5376,128]{1,0:T(8,128)(2,1)} async-done(((bf16[168,128]{1,0:T(8,128)(2,1)}), bf16[5376,128]{1,0:T(8,128)(2,1)}) %all-gather.9.cloned.1.call-update) | async-done | bytes 1376272 | tf_op jit(solution)/shard_map/all_gather | solution.py:65
  255.7 3.6 multiply_reduce_fusion.1
  259.7 4.2 collective-permute-start.4
  264.0 2.1 collective-permute-start.5
  266.1 2.4 collective-permute-start.6
  268.4 1.9 collective-permute-start.7
  270.4 74.8 %all-gather.7.cloned.1.call-done = bf16[5376,128]{1,0:T(8,128)(2,1)} async-done(((bf16[168,128]{1,0:T(8,128)(2,1)}), bf16[5376,128]{1,0:T(8,128)(2,1)}) %all-gather.7.cloned.1.call-update) | async-done | bytes 1376272 | tf_op jit(solution)/shard_map/all_gather | solution.py:66
  345.2 3.9 fusion.16
  349.1 4.2 collective-permute-start
  353.3 2.1 collective-permute-start.1
  356.3 2.4 collective-permute-start.2
  358.7 1.9 collective-permute-start.3
  366.7 3.0 copy.17
  369.7 3.7 multiply_reduce_fusion
  374.5 1.6 fusion.13
  376.1 67.2 %all-gather.11.cloned.1.call-done = bf16[256,5376]{0,1:T(8,128)(2,1)} async-done(((bf16[256,168]{0,1:T(8,128)(2,1)}), bf16[256,5376]{0,1:T(8,128)(2,1)}) %all-gather.11.cloned.1.call-update) | async-done | bytes 2752528 | tf_op jit(solution)/shard_map/all_gather | solution.py:97
  443.3 4.2 convolution_convert_fusion
  448.2 92.8 %reduce-scatter.2.cloned.1.call-done = bf16[256,336]{0,1:T(8,128)(2,1)} async-done(((bf16[256,5376]{0,1:T(8,128)(2,1)}), bf16[256,336]{0,1:T(8,128)(2,1)}) %reduce-scatter.2.cloned.1.call-update) | async-done | bytes 172048 | tf_op jit(solution)/shard_map/reduce_scatter | solution.py:100
  542.0 40.5 %psum.7 = f32[256]{0:T(256)S(1)} all-reduce(f32[256]{0:T(256)S(1)} %fusion.17), channel_id=1, replica_groups=mesh['seq'=32,'tensor'=16] {'tensor'}, use_global_device_ids=true, to_apply=%region_7.8 | all-reduce | flops 256 | bytes 2048 | tf_op jit(solution)/shard_map/psum | solution.py:103
  582.6 1.7 fusion.20
  (72 shorter events, 14.2 us)
Async XLA Ops:
  6.5 160.8 %all-gather.5.cloned.1.call-start = ((), (), s32[]{:S(2)}) async-start(), calls=%async_computation.2 | async-start | bytes 2924544 | tf_op jit(solution)/shard_map/all_gather | solution.py:54
  7.3 248.5 %all-gather.9.cloned.1.call-start = ((), (), s32[]{:S(2)}) async-start(), calls=%async_computation.4 | async-start | bytes 1419264 | tf_op jit(solution)/shard_map/all_gather | solution.py:65
  8.0 337.2 %all-gather.7.cloned.1.call-start = ((), (), s32[]{:S(2)}) async-start(), calls=%async_computation.3 | async-start | bytes 1419264 | tf_op jit(solution)/shard_map/all_gather | solution.py:66
  11.4 16.6 %copy-start.6 = (s32[256]{0:T(256)S(1)}, s32[256]{0:T(256)}, u32[]{:S(2)}) copy-start(s32[256]{0:T(256)} %param.11) | copy-start | bytes 3076
  11.4 16.7 %copy-start.8 = (f32[128]{0:T(128)S(1)}, f32[128]{0:T(128)}, u32[]{:S(2)}) copy-start(f32[128]{0:T(128)} %param.17) | copy-start | bytes 1540
  11.4 16.7 %copy-start.9 = (f32[128]{0:T(128)S(1)}, f32[128]{0:T(128)}, u32[]{:S(2)}) copy-start(f32[128]{0:T(128)} %param.16) | copy-start | bytes 1540
  11.4 16.7 %copy-start.1 = (f32[5376]{0:T(1024)S(1)}, f32[5376]{0:T(1024)}, u32[]{:S(2)}) copy-start(f32[5376]{0:T(1024)} %param.12) | copy-start | bytes 64516
  11.4 355.4 %all-to-all-start = ((bf16[32,168,256]{2,1,0:T(8,128)(2,1)}), bf16[32,168,256]{2,1,0:T(8,128)(2,1)S(1)}, u32[]{:S(2)}, u32[]{:S(2)}) async-start(bf16[32,168,256]{2,1,0:T(8,128)(2,1)} %stack.2), calls=%async_computation | async-start | bytes 5505024 | tf_op jit(solution)/shard_map/all_to_all | solution.py:62
  27.3 416.0 %all-gather.11.cloned.1.call-start = ((), (), s32[]{:S(2)}) async-start(), calls=%async_computation.5 | async-start | bytes 2838528 | tf_op jit(solution)/shard_map/all_gather | solution.py:97
  27.9 513.2 %reduce-scatter.2.cloned.1.call-start = ((), (), s32[]{:S(2)}) async-start(), calls=%async_computation.6 | async-start | bytes 2924544 | tf_op jit(solution)/shard_map/reduce_scatter | solution.py:100
  28.1 231.2 %copy-start.2 = (f32[5376]{0:T(1024)}, f32[5376]{0:T(1024)S(1)}, u32[]{:S(2)}) copy-start(f32[5376]{0:T(1024)S(1)} %broadcast_add_fusion) | copy-start | bytes 64516
  259.7 93.6 %collective-permute-start.4 = (bf16[256,1,128]{0,2,1:T(8,128)(2,1)S(1)}, bf16[256,1,128]{0,2,1:T(8,128)(2,1)}, u32[]{:S(2)}, u32[]{:S(2)}) collective-permute-start(bf16[256,1,128]{0,2,1:T(8,128)(2,1)S(1)} %pad_maximum_fusion), channel_id=1, source_target_pairs={{0,64},{16,80},{32,96},{48,112},{64,128},{80,144},{96,160},{112,17... | collective-permute-start | bytes 196616 | tf_op jit(solution)/shard_map/ppermute | solution.py:16
  264.0 92.3 %collective-permute-start.5 = (bf16[256,1,128]{0,2,1:T(8,128)(2,1)S(1)}, bf16[256,1,128]{0,2,1:T(8,128)(2,1)S(1)}, u32[]{:S(2)}, u32[]{:S(2)}) collective-permute-start(bf16[256,1,128]{0,2,1:T(8,128)(2,1)S(1)} %pad_maximum_fusion), channel_id=1, source_target_pairs={{0,48},{16,64},{32,80},{48,96},{64,112},{80,128},{96,144},{112,160... | collective-permute-start | bytes 196616 | tf_op jit(solution)/shard_map/ppermute | solution.py:16
  266.1 92.6 %collective-permute-start.6 = (bf16[256,1,128]{0,2,1:T(8,128)(2,1)S(1)}, bf16[256,1,128]{0,2,1:T(8,128)(2,1)S(1)}, u32[]{:S(2)}, u32[]{:S(2)}) collective-permute-start(bf16[256,1,128]{0,2,1:T(8,128)(2,1)S(1)} %pad_maximum_fusion), channel_id=1, source_target_pairs={{0,32},{16,48},{32,64},{48,80},{64,96},{80,112},{96,128},{112,144}... | collective-permute-start | bytes 196616 | tf_op jit(solution)/shard_map/ppermute | solution.py:16
  268.4 92.2 %collective-permute-start.7 = (bf16[256,1,128]{0,2,1:T(8,128)(2,1)S(1)}, bf16[256,1,128]{0,2,1:T(8,128)(2,1)S(1)}, u32[]{:S(2)}, u32[]{:S(2)}) collective-permute-start(bf16[256,1,128]{0,2,1:T(8,128)(2,1)S(1)} %pad_maximum_fusion), channel_id=1, source_target_pairs={{0,16},{16,32},{32,48},{48,64},{64,80},{80,96},{96,112},{112,128},... | collective-permute-start | bytes 196616 | tf_op jit(solution)/shard_map/ppermute | solution.py:16
  349.1 11.6 %collective-permute-start = (bf16[256,1,128]{2,0,1:T(8,128)(2,1)S(1)}, bf16[256,1,128]{2,0,1:T(8,128)(2,1)S(1)}, u32[]{:S(2)}, u32[]{:S(2)}) collective-permute-start(bf16[256,1,128]{2,0,1:T(8,128)(2,1)S(1)} %fusion.16), channel_id=1, source_target_pairs={{0,64},{16,80},{32,96},{48,112},{64,128},{80,144},{96,160},{112,17... | collective-permute-start | bytes 196616 | tf_op jit(solution)/shard_map/ppermute | solution.py:16
  353.3 8.3 %collective-permute-start.1 = (bf16[256,1,128]{2,0,1:T(8,128)(2,1)S(1)}, bf16[256,1,128]{2,0,1:T(8,128)(2,1)S(1)}, u32[]{:S(2)}, u32[]{:S(2)}) collective-permute-start(bf16[256,1,128]{2,0,1:T(8,128)(2,1)S(1)} %fusion.16), channel_id=1, source_target_pairs={{0,48},{16,64},{32,80},{48,96},{64,112},{80,128},{96,144},{112,160... | collective-permute-start | bytes 196616 | tf_op jit(solution)/shard_map/ppermute | solution.py:16
  356.3 7.6 %collective-permute-start.2 = (bf16[256,1,128]{2,0,1:T(8,128)(2,1)S(1)}, bf16[256,1,128]{2,0,1:T(8,128)(2,1)S(1)}, u32[]{:S(2)}, u32[]{:S(2)}) collective-permute-start(bf16[256,1,128]{2,0,1:T(8,128)(2,1)S(1)} %fusion.16), channel_id=1, source_target_pairs={{0,32},{16,48},{32,64},{48,80},{64,96},{80,112},{96,128},{112,144}... | collective-permute-start | bytes 196616 | tf_op jit(solution)/shard_map/ppermute | solution.py:16
  358.7 6.8 %collective-permute-start.3 = (bf16[256,1,128]{2,0,1:T(8,128)(2,1)S(1)}, bf16[256,1,128]{2,0,1:T(8,128)(2,1)S(1)}, u32[]{:S(2)}, u32[]{:S(2)}) collective-permute-start(bf16[256,1,128]{2,0,1:T(8,128)(2,1)S(1)} %fusion.16), channel_id=1, source_target_pairs={{0,16},{16,32},{32,48},{48,64},{64,80},{80,96},{96,112},{112,128},... | collective-permute-start | bytes 196616 | tf_op jit(solution)/shard_map/ppermute | solution.py:16
  360.6 5.4 copy-start.4
  366.7 3.0 copy-start.3
  369.7 3.9 copy-start.5
  447.6 0.7 copy-start.7
  447.6 135.0 %copy-start = (bf16[256,336]{0,1:T(8,128)(2,1)S(1)}, bf16[256,336]{0,1:T(8,128)(2,1)}, u32[]{:S(2)}) copy-start(bf16[256,336]{0,1:T(8,128)(2,1)} %param.10) | copy-start | bytes 516100
Sparse Core Ops, SparseCore 0:
  9.4 157.8 all-gather.4
  170.5 85.1 all-gather.8
  259.0 86.1 all-gather.6
  348.3 95.0 all-gather.10
  447.7 93.3 reduce-scatter.1
